TPU v7x, 512 devices: a whole 4x4x16 slice. The times are simulated.
512 devices in a mesh: ctx: 64 (over z, y_lo, core), tp: 8 (over x, y_hi).
Axes of the slice: x: 4, y: 4 (y_hi: 2, y_lo: 2; y = y_hi * 2 + y_lo), z: 16, core: 2. Of those that a mesh axis runs over, the one named last changes fastest.
Arguments:
- queries: bfloat16 [65536, 1024], P('ctx', 'tp'), may hold values from -6 to 6
- audio_keys: bfloat16 [2048, 1024], P('ctx', 'tp'), may hold values from -6 to 6
- audio_values: bfloat16 [2048, 1024], P('ctx', 'tp'), may hold values from -6 to 6
- grad_output: bfloat16 [65536, 1024], P('ctx', 'tp'), may hold values from -6 to 6
- out_weight: bfloat16 [1024, 1024], P('tp'), may hold values from -0.1875 to 0.1875
Outputs:
- grad_queries: bfloat16 [65536, 1024], P('ctx', 'tp')
- grad_keys: bfloat16 [2048, 1024], P('ctx', 'tp')
- grad_values: bfloat16 [2048, 1024], P('ctx', 'tp')
- grad_weight: float32 [1024, 1024], P('tp', 'ctx')
All inputs are finite; a program needn't handle non-finite values.
Results may differ from a plain program's by a relative error of at most 0.033.
Values may be sent and summed in bfloat16 or wider, within the bound.
A program may use at most 64 MiB of HBM per device.

v0:
```python
import math

import jax
import jax.numpy as jnp
from jax import lax
from jax.sharding import PartitionSpec as P

HD = 128


def key_sweep(step_fn, carried, key_rows, value_rows):
    row_count = key_rows.shape[0]
    block_rows = math.gcd(row_count, 512)

    def advance(counter, running):
        shift_rows = counter * block_rows
        key_block = lax.dynamic_slice_in_dim(key_rows, shift_rows, block_rows, 0)
        value_block = lax.dynamic_slice_in_dim(value_rows, shift_rows, block_rows, 0)
        return step_fn(running, key_block, value_block, shift_rows)

    return lax.fori_loop(0, row_count // block_rows, advance, carried)


def local(queries, audio_keys, audio_values, grad_output, out_weight):
    rows_here = queries.shape[0]
    head_count = queries.shape[1] // HD
    width_here = head_count * HD
    factor = 1.0 / math.sqrt(HD)
    query_heads = queries.reshape(rows_here, head_count, HD)
    whole_grad = lax.all_gather(grad_output, "tp", axis=1, tiled=True)
    grad_attended = jnp.einsum(
        "tc,ec->te", whole_grad, out_weight, preferred_element_type=jnp.float32
    ).astype(jnp.bfloat16)
    grad_heads = grad_attended.reshape(rows_here, head_count, HD)
    whole_keys, whole_values = (
        lax.all_gather(audio_keys, "ctx", axis=0, tiled=True),
        lax.all_gather(audio_values, "ctx", axis=0, tiled=True),
    )

    def scores_of(key_block):
        key_heads = key_block.reshape(key_block.shape[0], head_count, HD)
        scores = (
            jnp.einsum("thd,khd->htk", query_heads, key_heads, preferred_element_type=jnp.float32)
            * factor
        )
        return (scores, key_heads)

    def stat_step(running, key_block, value_block, offset):
        running_max, running_sum = running
        scores, key_heads = scores_of(key_block)
        new_max = jnp.maximum(running_max, jnp.max(scores, axis=-1))
        running_sum = running_sum * jnp.exp(running_max - new_max) + jnp.sum(
            jnp.exp(scores - new_max[..., None]), axis=-1
        )
        return (new_max, running_sum)

    stat_init = (
        jnp.full((head_count, rows_here), -1e30, jnp.float32),
        jnp.zeros((head_count, rows_here), jnp.float32),
    )
    running_max, running_sum = key_sweep(stat_step, stat_init, whole_keys, whole_values)
    logsum = running_max + jnp.log(running_sum)

    def attend_step(running, key_block, value_block, offset):
        scores, key_heads = scores_of(key_block)
        value_heads = value_block.reshape(value_block.shape[0], head_count, HD)
        probs = jnp.exp(scores - logsum[..., None]).astype(jnp.bfloat16)
        return running + jnp.einsum(
            "htk,khd->thd", probs, value_heads, preferred_element_type=jnp.float32
        )

    attend_init = jnp.zeros((rows_here, head_count, HD), jnp.float32)
    attended = key_sweep(attend_step, attend_init, whole_keys, whole_values).astype(jnp.bfloat16)
    row_delta = jnp.sum(grad_heads.astype(jnp.float32) * attended.astype(jnp.float32), axis=-1).T
    weight_term = jnp.einsum(
        "te,tc->ec",
        attended.reshape(rows_here, width_here),
        whole_grad,
        preferred_element_type=jnp.float32,
    )
    grad_weight = lax.psum_scatter(weight_term, "ctx", scatter_dimension=1, tiled=True)

    def make_back():

        def back_step(running, key_block, value_block, offset):
            query_acc, key_buffer, value_buffer = running
            block_rows = key_block.shape[0]
            scores, key_heads = scores_of(key_block)
            value_heads = value_block.reshape(block_rows, head_count, HD)
            probs = jnp.exp(scores - logsum[..., None]).astype(jnp.bfloat16)
            grad_probs = jnp.einsum(
                "thd,khd->htk", grad_heads, value_heads, preferred_element_type=jnp.float32
            )
            grad_scores = (probs.astype(jnp.float32) * (grad_probs - row_delta[..., None])).astype(
                jnp.bfloat16
            )
            query_acc = (
                query_acc
                + jnp.einsum(
                    "htk,khd->thd", grad_scores, key_heads, preferred_element_type=jnp.float32
                )
                * factor
            )
            key_part = (
                jnp.einsum(
                    "htk,thd->khd", grad_scores, query_heads, preferred_element_type=jnp.float32
                )
                * factor
            )
            value_part = jnp.einsum(
                "htk,thd->khd", probs, grad_heads, preferred_element_type=jnp.float32
            )
            key_old = lax.dynamic_slice_in_dim(key_buffer, offset, block_rows, 0)
            value_old = lax.dynamic_slice_in_dim(value_buffer, offset, block_rows, 0)
            key_buffer = lax.dynamic_update_slice_in_dim(
                key_buffer, key_old + key_part.reshape(block_rows, width_here), offset, 0
            )
            value_buffer = lax.dynamic_update_slice_in_dim(
                value_buffer, value_old + value_part.reshape(block_rows, width_here), offset, 0
            )
            return (query_acc, key_buffer, value_buffer)

        return back_step

    query_zeros = jnp.zeros((rows_here, head_count, HD), jnp.float32)
    buffer_zeros = jnp.zeros((whole_keys.shape[0], width_here), jnp.float32)
    query_acc, key_buffer, value_buffer = key_sweep(
        make_back(), (query_zeros, buffer_zeros, buffer_zeros), whole_keys, whole_values
    )
    key_sum, value_sum = (
        lax.psum_scatter(key_buffer, "ctx", scatter_dimension=0, tiled=True),
        lax.psum_scatter(value_buffer, "ctx", scatter_dimension=0, tiled=True),
    )
    grad_queries = query_acc.astype(jnp.bfloat16).reshape(rows_here, width_here)
    return (grad_queries, key_sum.astype(jnp.bfloat16), value_sum.astype(jnp.bfloat16), grad_weight)


def solution(mesh):
    return jax.shard_map(
        local,
        mesh=mesh,
        in_specs=(P("ctx", "tp"), P("ctx", "tp"), P("ctx", "tp"), P("ctx", "tp"), P("tp", None)),
        out_specs=(P("ctx", "tp"), P("ctx", "tp"), P("ctx", "tp"), P("tp", "ctx")),
        check_vma=False,
    )
```

profile of v0, /device:TPU:6, one launch (start us, length us, event | category | flops | bytes accessed | tf_op | source)
XLA Modules:
  0.0 862.4 jit_solution(5510867804520159809)
XLA Ops:
  7.2 0.7 all-gather.2.cloned.1.call-update
  8.0 71.7 %all_gather.9 = bf16[2048,128]{1,0:T(8,128)(2,1)S(1)} all-gather(bf16[32,128]{1,0:T(8,128)(2,1)} %param.12), channel_id=1, replica_groups=mesh['ctx'=64,'tp'=8] {'ctx'}, dimensions={0}, use_global_device_ids=true | all-gather | bytes 532480 | tf_op jit(solution)/shard_map/all_gather | solution.py:36
  79.7 7.4 while.48
  79.7 1.4 multiply_reduce_fusion.3
  81.2 0.4 exponential_reduce_fusion.2
  81.6 1.4 multiply_reduce_fusion.3
  83.0 0.4 exponential_reduce_fusion.2
  83.4 1.4 multiply_reduce_fusion.3
  85.3 1.4 multiply_reduce_fusion.3
  87.2 61.0 %all_gather.10 = bf16[2048,128]{1,0:T(8,128)(2,1)S(1)} all-gather(bf16[32,128]{1,0:T(8,128)(2,1)S(1)} %copy-done.8), channel_id=1, replica_groups=mesh['ctx'=64,'tp'=8] {'ctx'}, dimensions={0}, use_global_device_ids=true | all-gather | bytes 532480 | tf_op jit(solution)/shard_map/all_gather | solution.py:37
  148.1 6.8 while.49
  148.2 1.7 fusion.69
  149.8 1.7 fusion.69
  151.5 1.7 fusion.69
  153.2 1.7 fusion.69
  155.0 0.8 copy-done.4
  155.7 2.4 multiply_reduce_fusion.1
  158.5 0.6 copy-done.1
  159.1 19.9 %while.50 = (s32[]{:T(128)}, f32[1024,1,128]{0,2,1:T(8,128)S(1)}, f32[2048,128]{1,0:T(8,128)S(1)}, f32[2048,128]{1,0:T(8,128)S(1)}, bf16[2048,128]{1,0:T(8,128)(...) while((s32[]{:T(128)}, f32[1024,1,128]{0,2,1:T(8,128)S(1)}, ...), condition=%wide.region_8.0_spmd.clone, body=%wide.region_7.0_spmd.clone.sunk | while | flops 675348480 | bytes 9838809 | solution.py:21
  159.1 1.4 exponential_convert_fusion.3
  160.5 1.3 multiply_convert_fusion.2
  161.9 0.4 fusion.82
  162.3 1.3 fusion.80
  163.6 0.4 fusion.81
  164.1 1.4 exponential_convert_fusion.3
  165.5 1.3 multiply_convert_fusion.2
  166.9 0.4 fusion.82
  167.3 1.3 fusion.80
  168.6 0.4 fusion.81
  169.1 1.4 exponential_convert_fusion.3
  170.5 1.3 multiply_convert_fusion.2
  171.9 0.4 fusion.82
  172.3 1.3 fusion.80
  173.6 0.4 fusion.81
  174.1 1.4 exponential_convert_fusion.3
  175.5 1.3 multiply_convert_fusion.2
  176.8 0.4 fusion.82
  177.3 1.3 fusion.80
  178.6 0.4 fusion.81
  179.1 1.0 copy-done.2
  180.4 0.4 reduce-scatter.4.cloned.1.call-update
  180.9 3.3 fusion.36
  184.2 0.8 copy.12
  185.1 217.4 %reduce-scatter.6.cloned.1.call-done = f32[32,128]{1,0:T(8,128)} async-done(((f32[2048,128]{1,0:T(8,128)}), f32[32,128]{1,0:T(8,128)}) %reduce-scatter.6.cloned.1.call-update) | async-done | bytes 16400 | tf_op jit(solution)/shard_map/reduce_scatter | solution.py:132
  402.5 1.3 convert_element_type.64
  403.8 225.6 %reduce-scatter.4.cloned.1.call-done = f32[32,128]{1,0:T(8,128)} async-done(((f32[2048,128]{1,0:T(8,128)}), f32[32,128]{1,0:T(8,128)}) %reduce-scatter.4.cloned.1.call-update) | async-done | bytes 16400 | tf_op jit(solution)/shard_map/reduce_scatter | solution.py:131
  629.4 1.3 convert_element_type.63
  630.7 225.1 %reduce-scatter.8.cloned.1.call-done = f32[128,16]{0,1:T(8,128)} async-done(((f32[128,1024]{0,1:T(8,128)}), f32[128,16]{0,1:T(8,128)}) %reduce-scatter.8.cloned.1.call-update) | async-done | bytes 8208 | tf_op jit(solution)/shard_map/reduce_scatter | solution.py:81
  (44 shorter events, 1.7 us)
Async XLA Ops:
  7.2 148.6 %copy-start = (bf16[128,1024]{1,0:T(8,128)(2,1)S(1)}, bf16[128,1024]{1,0:T(8,128)(2,1)}, u32[]{:S(2)}) copy-start(bf16[128,1024]{1,0:T(8,128)(2,1)} %param.15) | copy-start | bytes 786436
  7.2 147.8 %all-gather.2.cloned.1.call-start = ((), (), s32[]{:S(2)}) async-start(), calls=%async_computation.3 | async-start | bytes 2359296 | tf_op jit(solution)/shard_map/all_gather | solution.py:30
  7.9 394.6 %reduce-scatter.6.cloned.1.call-start = ((), (), s32[]{:S(2)}) async-start(), calls=%async_computation.5 | async-start | bytes 1064960 | tf_op jit(solution)/shard_map/reduce_scatter | solution.py:132
  79.7 7.4 copy-start.8
  154.9 0.8 copy-start.4
  154.9 3.4 copy-start.6
  154.9 3.4 copy-start.5
  158.2 1.0 copy-start.1
  179.1 1.0 copy-start.2
  179.1 1.3 copy-start.3
  179.1 1.8 copy-start.7
  180.1 449.3 %reduce-scatter.4.cloned.1.call-start = ((), (), s32[]{:S(2)}) async-start(), calls=%async_computation.4 | async-start | bytes 1064960 | tf_op jit(solution)/shard_map/reduce_scatter | solution.py:131
  180.8 675.1 %reduce-scatter.8.cloned.1.call-start = ((), (), s32[]{:S(2)}) async-start(), calls=%async_computation.6 | async-start | bytes 532480 | tf_op jit(solution)/shard_map/reduce_scatter | solution.py:81
Sparse Core Ops, SparseCore 0:
  11.1 77.9 all-gather.1
  180.2 222.2 reduce-scatter.5
  405.5 223.8 reduce-scatter.3
  632.6 223.1 reduce-scatter.7
where the time goes:
time: 863 us; the launch traced here: 862 us
  waiting for transfers between devices  669 us (78%)
  blocking collectives  133 us (15%)
  matrix products  37.8 us (4%)
  between operations  14 us (2%)
    reduce_scatter x1, waiting for transfers between devices, local(): lax.psum_scatter(key_buffer, 'ctx', scatter_dimension=0, tiled=True)  226 us
    reduce_scatter x1, waiting for transfers between devices, local(): lax.psum_scatter(weight_term, 'ctx', scatter_dimension=1, tiled=True)  225 us
    reduce_scatter x1, waiting for transfers between devices, local(): lax.psum_scatter(value_buffer, 'ctx', scatter_dimension=0, tiled=True)  217 us
    all_gather x1, blocking collectives, local(): lax.all_gather(audio_keys, 'ctx', axis=0, tiled=True)  71.7 us
    all_gather x1, blocking collectives, local(): lax.all_gather(audio_values, 'ctx', axis=0, tiled=True)  61 us
  transfers between devices with their start and end apart: 4, of which 3 were waited for; matrix products, arithmetic and copies ran while one was open for 2% of the time, Pallas kernels for 0%

commit v1 on v0

v1 whole, which is shorter than its diff:
```python
import functools
import math

import jax
import jax.numpy as jnp
from jax import lax
from jax.experimental import pallas as pl
from jax.experimental.pallas import tpu as pltpu
from jax.sharding import PartitionSpec as P

MESH = pl.DeviceIdType.MESH
F32, BF16 = jnp.float32, jnp.bfloat16
HD = 128
ROWS = 1024
GROUP = 512
PARTS = 4
PART = ROWS // PARTS
FACTOR = 1.0 / math.sqrt(HD)
LOG2E = math.log2(math.e)
OFFSETS = (2, 1, 3, 0)
TP_SHIFTS = tuple((a, b) for a in range(4) for b in range(2) if a or b)


def nn(a, b):
    return lax.dot_general(a, b, (((1,), (0,)), ((), ())), preferred_element_type=F32)


def nt(a, b):
    return lax.dot_general(a, b, (((1,), (1,)), ((), ())), preferred_element_type=F32)


def tn(a, b):
    return lax.dot_general(a, b, (((0,), (0,)), ((), ())), preferred_element_type=F32)


def kernel(
    q_ref, k_ref, v_ref, g_ref, w_ref,
    dq_ref, dk_ref, dv_ref, dw_ref,
    kv, gall, scores, probs, att_t, da_t, da, dq_t, acc, keep,
    s1, r1, s2, r2, s3, r3, s4, r4, tot,
    za_s, za_r, zb_s, zb_r, ya_s, ya_r, ca_s, ca_r, g_s, g_r,
    c1_s, c1_r, y2_s, y2_r, z3_s, z3_r, z4_s, z4_r,
):
    ctx, tp = lax.axis_index("ctx"), lax.axis_index("tp")
    z, yl, core = ctx // 4, (ctx // 2) % 2, ctx % 2
    zh, zl = z // 4, z % 4

    def on_ctx(dz=0, dy=0, dc=0):
        there = ((z + dz) % 16) * 4 + ((yl + dy) % 2) * 2 + (core + dc) % 2
        return (there, tp)

    def on_tp(dx, dy):
        return (ctx, ((tp // 2 + dx) % 4) * 2 + (tp % 2 + dy) % 2)

    def copy(src, dst, ssem, rsem, to):
        return pltpu.make_async_remote_copy(
            src_ref=src, dst_ref=dst, send_sem=ssem, recv_sem=rsem, device_id=to, device_id_type=MESH
        )

    barrier = pltpu.get_barrier_semaphore()
    greeted = [on_ctx(dc=1), on_ctx(dy=1)]
    greeted += [on_ctx(dz=d) for d in (1, 15, 2, 14, 4, 8, 12)]
    greeted += [on_tp(*d) for d in TP_SHIFTS]
    for there in greeted:
        pl.semaphore_signal(barrier, inc=1, device_id=there, device_id_type=MESH)
    kv[zl, 0, core, yl, pl.ds(zh * 32, 32)] = k_ref[...]
    kv[zl, 1, core, yl, pl.ds(zh * 32, 32)] = v_ref[...]
    gall[tp] = g_ref[...]
    pl.semaphore_wait(barrier, len(greeted))

    sends = []

    def go(c):
        c.start()
        sends.append(c)
        return c

    own = kv.at[zl, :, core, yl, pl.ds(zh * 32, 32)]
    far = [
        go(copy(own, own, za_s.at[i], za_r.at[i], on_ctx(dz=4 * (i + 1)))) for i in range(3)
    ]
    gcopies = {}

    def send_grad(part):
        rows = pl.ds(part * PART, PART)
        for i, d in enumerate(TP_SHIFTS):
            gcopies[i, part] = go(
                copy(g_ref.at[rows], gall.at[tp, rows], g_s.at[i, part], g_r.at[i, part], on_tp(*d))
            )

    send_grad(0)
    send_grad(1)
    for c in far:
        c.wait_recv()
    piece = kv.at[zl, :, core, yl]
    near = [
        go(copy(piece, piece, zb_s.at[i], zb_r.at[i], on_ctx(dz=d))) for i, d in enumerate((2, 1, 15))
    ]
    order = ((zl, None), ((zl + 3) % 4, 1), ((zl + 1) % 4, 2), ((zl + 2) % 4, 0))
    across, swap = [], []
    for i, (r, src) in enumerate(order):
        if src is not None:
            near[src].wait_recv()
        p = kv.at[r, :, core, yl]
        across.append(go(copy(p, p, ya_s.at[i], ya_r.at[i], on_ctx(dy=1))))
        if i == 0:
            send_grad(2)
            send_grad(3)
    for i, (r, _) in enumerate(order):
        across[i].wait_recv()
        p = kv.at[r, :, core]
        swap.append(go(copy(p, p, ca_s.at[i], ca_r.at[i], on_ctx(dc=1))))

    top = jnp.full((8, ROWS), -jnp.inf, F32)
    for i, (r, _) in enumerate(order):
        swap[i].wait_recv()
        for h in range(2):
            kb = kv[r, 0, h].reshape(256, HD)
            s = nt(kb, q_ref[...])
            scores[i, pl.ds(h * 256, 256)] = s
            top = jnp.maximum(top, jnp.max(s.reshape(32, 8, ROWS), axis=0))
    shift = jnp.max(top, axis=0, keepdims=True) * (FACTOR * LOG2E)
    total = jnp.zeros((8, ROWS), F32)
    acc_t = jnp.zeros((HD, ROWS), F32)
    for i, (r, _) in enumerate(order):
        for h in range(2):
            vb = kv[r, 1, h].reshape(256, HD)
            e = jnp.exp2(scores[i, pl.ds(h * 256, 256)] * (FACTOR * LOG2E) - shift)
            total = total + jnp.sum(e.reshape(32, 8, ROWS), axis=0)
            eb = e.astype(BF16)
            probs[i, pl.ds(h * 256, 256)] = eb
            acc_t = acc_t + tn(vb, eb)
    inverse = 1.0 / jnp.sum(total, axis=0, keepdims=True)
    att_t[...] = (acc_t * inverse).astype(BF16)

    for part in range(PARTS):
        for i in range(len(TP_SHIFTS)):
            gcopies[i, part].wait_recv()
    x_t = jnp.zeros((HD, ROWS), F32)
    for b in range(8):
        x_t = x_t + nt(w_ref[:, b * 128 : (b + 1) * 128], gall[b])
    x_t = x_t * inverse
    delta = jnp.sum(x_t * att_t[...].astype(F32), axis=0, keepdims=True)
    da_t[...] = x_t.astype(BF16)
    da[...] = x_t.T.astype(BF16)

    for b in range(8):
        part_w = nn(att_t[...], gall[b]).T
        for j in range(8):
            zz, o = 2 * b + j // 4, j % 4
            g = (zz % 4 - zl + 4) % 4
            slot = jnp.where(g == 2, 0, jnp.where(g == 1, 1, jnp.where(g == 3, 2, 3)))
            acc[slot, o % 2, o // 2, pl.ds(256 + (zz // 4) * 16, 16)] = part_w[j * 16 : (j + 1) * 16]

    position = {2: 3, 1: 2, 3: 1, 0: 0}
    dq_t[...] = jnp.zeros((HD, ROWS), F32)
    first, second, third = [None] * 4, [None] * 4, [None] * 3

    def compute(g):
        r = (zl + OFFSETS[g]) % 4
        i = position[OFFSETS[g]]
        for h in range(2):
            kb = kv[r, 0, h].reshape(256, HD)
            vb = kv[r, 1, h].reshape(256, HD)
            pb = probs[i, pl.ds(h * 256, 256)]
            ds = (pb.astype(F32) * (nn(vb, da_t[...]) - delta)).astype(BF16)
            acc[g, h, :, pl.ds(0, 128)] = (nn(ds, q_ref[...]) * FACTOR).reshape(2, 128, HD)
            acc[g, h, :, pl.ds(128, 128)] = nn(pb, da[...]).reshape(2, 128, HD)
            dq_t[...] += tn(kb, ds)
        s1[g] = acc[g, 1 - core].astype(BF16)
        first[g] = go(copy(s1.at[g], r1.at[g], c1_s.at[g], c1_r.at[g], on_ctx(dc=1)))

    def step_y(g):
        first[g].wait_recv()
        s2[g] = (acc[g, core, 1 - yl] + r1[g, 1 - yl].astype(F32)).astype(BF16)
        second[g] = go(copy(s2.at[g], r2.at[g], y2_s.at[g], y2_r.at[g], on_ctx(dy=1)))
        keep[g] = acc[g, core, yl] + r1[g, yl].astype(F32)

    def step_z(g):
        second[g].wait_recv()
        if g == 3:
            tot[...] = keep[g] + r2[g].astype(F32)
        else:
            s3[g] = (keep[g] + r2[g].astype(F32)).astype(BF16)
            there = on_ctx(dz=(2, 1, 15)[g])
            third[g] = go(copy(s3.at[g], r3.at[g], z3_s.at[g], z3_r.at[g], there))

    for g in range(4):
        compute(g)
        if g >= 1:
            step_y(g - 1)
        if g >= 2:
            step_z(g - 2)
    step_y(3)
    step_z(2)
    dq_ref[...] = (dq_t[...] * FACTOR).T.astype(BF16)
    step_z(3)
    for c in third:
        c.wait_recv()
    tot[...] += (r3[0].astype(F32) + r3[1].astype(F32)) + r3[2].astype(F32)

    def cut(h):
        return (
            tot[pl.ds(h * 32, 32)],
            tot[pl.ds(128 + h * 32, 32)],
            tot[pl.ds(256 + h * 16, 16)],
        )

    last = []
    for i in range(3):
        a, b, c = cut((zh + i + 1) % 4)
        s4[i, 0:32] = a.astype(BF16)
        s4[i, 32:64] = b.astype(BF16)
        s4[i, 64:80] = c.astype(BF16)
        last.append(
            go(copy(s4.at[i], r4.at[i], z4_s.at[i], z4_r.at[i], on_ctx(dz=4 * (i + 1))))
        )
    a, b, c = cut(zh)
    for copy_in in last:
        copy_in.wait_recv()
    more = (r4[0].astype(F32) + r4[1].astype(F32)) + r4[2].astype(F32)
    dk_ref[...] = (a + more[0:32]).astype(BF16)
    dv_ref[...] = (b + more[32:64]).astype(BF16)
    dw_ref[...] = c + more[64:80]
    for c in sends:
        c.wait_send()


def local(queries, audio_keys, audio_values, grad_output, out_weight):
    vmem = pl.BlockSpec(memory_space=pltpu.VMEM)
    dma = lambda *n: pltpu.SemaphoreType.DMA(n)
    scratch = [
        pltpu.VMEM((4, 2, 2, 2, 128, HD), BF16),
        pltpu.VMEM((8, ROWS, 128), BF16),
        pltpu.VMEM((4, GROUP, ROWS), F32),
        pltpu.VMEM((4, GROUP, ROWS), BF16),
        pltpu.VMEM((HD, ROWS), BF16),
        pltpu.VMEM((HD, ROWS), BF16),
        pltpu.VMEM((ROWS, HD), BF16),
        pltpu.VMEM((HD, ROWS), F32),
        pltpu.VMEM((4, 2, 2, 320, HD), F32),
        pltpu.VMEM((4, 320, HD), F32),
        pltpu.VMEM((4, 2, 320, HD), BF16),
        pltpu.VMEM((4, 2, 320, HD), BF16),
        pltpu.VMEM((4, 320, HD), BF16),
        pltpu.VMEM((4, 320, HD), BF16),
        pltpu.VMEM((3, 320, HD), BF16),
        pltpu.VMEM((3, 320, HD), BF16),
        pltpu.VMEM((3, 80, HD), BF16),
        pltpu.VMEM((3, 80, HD), BF16),
        pltpu.VMEM((320, HD), F32),
        dma(3), dma(3), dma(3), dma(3), dma(4), dma(4), dma(4), dma(4), dma(7, PARTS), dma(7, PARTS),
        dma(4), dma(4), dma(4), dma(4), dma(3), dma(3), dma(3), dma(3),
    ]
    dq, dk, dv, dw = pl.pallas_call(
        kernel,
        out_shape=(
            jax.ShapeDtypeStruct((ROWS, HD), BF16),
            jax.ShapeDtypeStruct((32, HD), BF16),
            jax.ShapeDtypeStruct((32, HD), BF16),
            jax.ShapeDtypeStruct((16, HD), F32),
        ),
        in_specs=[vmem] * 5,
        out_specs=(vmem,) * 4,
        scratch_shapes=scratch,
        compiler_params=pltpu.CompilerParams(
            collective_id=0, has_side_effects=True, vmem_limit_bytes=48 * 2**20
        ),
    )(queries, audio_keys, audio_values, grad_output, out_weight)
    return dq, dk, dv, dw.T


def solution(mesh):
    return jax.shard_map(
        local,
        mesh=mesh,
        in_specs=(P("ctx", "tp"), P("ctx", "tp"), P("ctx", "tp"), P("ctx", "tp"), P("tp", None)),
        out_specs=(P("ctx", "tp"), P("ctx", "tp"), P("ctx", "tp"), P("tp", "ctx")),
        check_vma=False,
    )
```

time: 863 us -> 80.8 us (0.09)
  waiting for transfers between devices: 669 us -> 0 us
  blocking collectives: 133 us -> 0 us
  Pallas kernels: 0 us -> 71.9 us
  matrix products: 37.8 us -> 0 us
  between operations: 14 us -> 0.65 us
    reduce_scatter x3 -> x0, waiting for transfers between devices: 668 us -> none  [the longest x1 226 us: local(): lax.psum_scatter(key_buffer, 'ctx', scatter_dimension=0, tiled=True)]
    all_gather x2 -> x0, blocking collectives: 133 us -> none  [the longest x1 71.7 us: local(): lax.all_gather(audio_keys, 'ctx', axis=0, tiled=True)]
    pallas_call x0 -> x1, Pallas kernels: none -> 71.9 us  [local(): pl.pallas_call(kernel, out_shape=(jax.ShapeDtypeStruct((ROWS, HD), BF16),...]
    dot_general x30 -> x0, matrix products: 37.8 us -> none  [the longest x8 11.2 us: scores_of(): jnp.einsum('thd,khd->htk', query_heads, key_heads, preferred_element_type...]
  transfers between devices with their start and end apart: 4 -> 0, of which waited for: 3 -> 0; matrix products, arithmetic and copies ran while one was open for 2% -> 0% of each run, Pallas kernels for 0% -> 0%
where the time goes in v1:
time: 80.8 us; the launch traced here: 79.3 us
  Pallas kernels  71.9 us (89%)
  local copies, waits for them, and re-layouts  6.73 us (8%)
    pallas_call x1, Pallas kernels, local(): pl.pallas_call(kernel, out_shape=(jax.ShapeDtypeStruct((ROWS, HD), BF16),...  71.9 us
    unnamed x14, local copies, waits for them, and re-layouts  6.73 us

profile of v1, /device:TPU:6, one launch (start us, length us, event | category | flops | bytes accessed | tf_op | source)
XLA Modules:
  0.0 79.3 jit_solution(12953276712880947578)
XLA Ops:
  0.6 0.0 copy-start
  0.6 0.9 %copy-done = bf16[1024,128]{1,0:T(8,128)(2,1)S(1)} copy-done((bf16[1024,128]{1,0:T(8,128)(2,1)S(1)}, bf16[1024,128]{1,0:T(8,128)(2,1)}, u32[]{:S(2)}) %copy-start) | copy-done | bytes 262168
  1.6 0.0 copy-start.1
  1.6 0.9 %copy-done.1 = bf16[1024,128]{1,0:T(8,128)(2,1)S(1)} copy-done((bf16[1024,128]{1,0:T(8,128)(2,1)S(1)}, bf16[1024,128]{1,0:T(8,128)(2,1)}, u32[]{:S(2)}) %copy-start.1) | copy-done | bytes 262168
  2.5 0.0 copy-start.2
  2.5 0.9 %copy-done.2 = bf16[128,1024]{1,0:T(8,128)(2,1)S(1)} copy-done((bf16[128,1024]{1,0:T(8,128)(2,1)S(1)}, bf16[128,1024]{1,0:T(8,128)(2,1)}, u32[]{:S(2)}) %copy-start.2) | copy-done | bytes 262168
  3.5 0.0 copy-start.3
  3.5 0.7 copy-done.3
  4.2 0.0 copy-start.4
  4.2 0.7 copy-done.4
  4.9 71.9 %shard_map.84 = (bf16[1024,128]{1,0:T(8,128)(2,1)S(1)}, bf16[32,128]{1,0:T(8,128)(2,1)S(1)}, bf16[32,128]{1,0:T(8,128)(2,1)S(1)}, f32[16,128]{1,0:T(8,128)S(1)}) custom-call(bf16[1024,128]{1,0:T(8,128)(2,1)S(1)} %copy-done, bf16[32,128]{1,0:T(8,128)(2,1)S(1)} %copy-done.3, bf16[32,128]{1,0:T(8,128)(2,1)S(1)} %copy-done.4, bf16[1024,128]{1,0:T(8,128)(2,1)S(1)} %copy-done.1, ...), custom_call_target="tpu_custom_call" | custom-call | tf_op jit(solution)/shard_map/pallas_call | solution.py:255
  76.8 0.7 copy.13
  77.5 0.6 copy.14
  78.1 0.6 copy.15
  78.7 0.6 copy.16
Async XLA Ops:
  0.6 1.0 %copy-start = (bf16[1024,128]{1,0:T(8,128)(2,1)S(1)}, bf16[1024,128]{1,0:T(8,128)(2,1)}, u32[]{:S(2)}) copy-start(bf16[1024,128]{1,0:T(8,128)(2,1)} %q_ref.1) | copy-start | bytes 786436
  1.6 0.9 %copy-start.1 = (bf16[1024,128]{1,0:T(8,128)(2,1)S(1)}, bf16[1024,128]{1,0:T(8,128)(2,1)}, u32[]{:S(2)}) copy-start(bf16[1024,128]{1,0:T(8,128)(2,1)} %g_ref.1) | copy-start | bytes 786436
  2.5 0.9 %copy-start.2 = (bf16[128,1024]{1,0:T(8,128)(2,1)S(1)}, bf16[128,1024]{1,0:T(8,128)(2,1)}, u32[]{:S(2)}) copy-start(bf16[128,1024]{1,0:T(8,128)(2,1)} %w_ref.1) | copy-start | bytes 786436
  3.5 0.7 copy-start.3
  4.2 0.7 copy-start.4

commit v2 on v1

v2 whole, which is shorter than its diff:
```python
import math

import jax
import jax.numpy as jnp
from jax import lax
from jax.experimental import pallas as pl
from jax.experimental.pallas import tpu as pltpu
from jax.sharding import PartitionSpec as P

MESH = pl.DeviceIdType.MESH
F32, BF16 = jnp.float32, jnp.bfloat16
HD = 128
ROWS = 1024
CHUNK = 512
KEYS = 32
SLOT = 80
PARTS = 4
PART = ROWS // PARTS
FACTOR = 1.0 / math.sqrt(HD)
LOG2E = math.log2(math.e)
NEAR = (0, 1, 2, 15)
FORTH = (0, 1, 3, 2)
BACK = (2, 1, 3, 0)
SPOTS = [(e, i) for i in (2, 1, 3, 0) for e in range(2) if i or e]


def nn(a, b):
    return lax.dot_general(a, b, (((1,), (0,)), ((), ())), preferred_element_type=F32)


def nt(a, b):
    return lax.dot_general(a, b, (((1,), (1,)), ((), ())), preferred_element_type=F32)


def tn(a, b):
    return lax.dot_general(a, b, (((0,), (0,)), ((), ())), preferred_element_type=F32)


def kernel(
    q_hbm, k_hbm, v_hbm, g_hbm, w_hbm,
    dq_ref, dk_ref, dv_ref, dw_ref,
    q_ref, w_ref, kv, gall, scores, probs, att_t, da_t, da, dq_t, acc,
    s1, r1, s3, r3, s4, r4,
    in_s, far_s, far_r, near_s, near_r, ca_s, ca_r, g_s, g_r,
    c1_s, c1_r, m_s, m_r, z4_s, z4_r,
):
    ctx, tp = lax.axis_index("ctx"), lax.axis_index("tp")
    z, yl, core = ctx // 4, (ctx // 2) % 2, ctx % 2

    def on_ctx(dz=0, dy=0, dc=0):
        there = ((z + dz) % 16) * 4 + ((yl + dy) % 2) * 2 + (core + dc) % 2
        return (there, tp)

    def on_tp(dx, dy):
        return (ctx, ((tp // 2 + dx) % 4) * 2 + (tp % 2 + dy) % 2)

    def copy(src, dst, ssem, rsem, to):
        return pltpu.make_async_remote_copy(
            src_ref=src, dst_ref=dst, send_sem=ssem, recv_sem=rsem, device_id=to, device_id_type=MESH
        )

    own = kv.at[0, :, 0, 0, 0]
    loads = [
        pltpu.make_async_copy(k_hbm, own.at[0], in_s.at[0]),
        pltpu.make_async_copy(v_hbm, own.at[1], in_s.at[1]),
        pltpu.make_async_copy(g_hbm, gall.at[tp], in_s.at[2]),
        pltpu.make_async_copy(q_hbm, q_ref, in_s.at[3]),
        pltpu.make_async_copy(w_hbm, w_ref, in_s.at[4]),
    ]
    for c in loads:
        c.start()
    barrier = pltpu.get_barrier_semaphore()
    greeted = [on_ctx(dc=1), on_ctx(dy=1)]
    greeted += [on_ctx(dz=d, dy=e) for d in (1, 15, 2, 14) for e in range(2)]
    greeted += [on_ctx(dz=d) for d in (4, 8, 12)]
    greeted += [on_tp(0, 1), on_tp(1, 0), on_tp(3, 0)]
    for there in greeted:
        pl.semaphore_signal(barrier, inc=1, device_id=there, device_id_type=MESH)
    for c in loads:
        c.wait()
    pl.semaphore_wait(barrier, len(greeted))

    sends = []

    def go(c):
        c.start()
        sends.append(c)
        return c

    far = {
        k: go(copy(own, kv.at[k, :, 0, 0, 0], far_s.at[k], far_r.at[k], on_ctx(dz=4 * k)))
        for k in (2, 1, 3)
    }
    near = {}

    def send_near(k):
        if k:
            far[k].wait_recv()
        for e, i in SPOTS:
            near[k, e, i] = go(
                copy(
                    kv.at[k, :, 0, 0, 0],
                    kv.at[k, :, 0, e, i],
                    near_s.at[k, e, i],
                    near_r.at[k, e, i],
                    on_ctx(dz=NEAR[i], dy=e),
                )
            )

    swap = {}

    def send_swap(k):
        for e, i in SPOTS:
            near[k, e, i].wait_recv()
        swap[k] = go(copy(kv.at[k, :, 0], kv.at[k, :, 1], ca_s.at[k], ca_r.at[k], on_ctx(dc=1)))

    send_near(0)

    gc = {}

    def send_grad(i, part, dx_from, dy_from, dx, dy):
        rows = pl.ds(part * PART, PART)
        b = gall.at[((tp // 2 + dx_from) % 4) * 2 + (tp % 2 + dy_from) % 2, rows]
        gc[i, part] = go(copy(b, b, g_s.at[i, part], g_r.at[i, part], on_tp(dx, dy)))

    waited = set()

    def arrived(i, part):
        if (i, part) not in waited:
            gc[i, part].wait_recv()
            waited.add((i, part))

    def relay_y(part):
        arrived(0, part)
        send_grad(3, part, 0, 1, 1, 0)
        send_grad(4, part, 0, 1, 3, 0)

    def relay_x(part, dy):
        if part % 2 == 0:
            arrived(1 + 2 * dy, part)
            send_grad(5 + dy, part, 3, dy, 1, 0)
        else:
            arrived(2 + 2 * dy, part)
            send_grad(5 + dy, part, 1, dy, 3, 0)

    def relay_late(part):
        arrived(1, part)
        send_grad(3, part, 3, 0, 0, 1)
        arrived(2, part)
        send_grad(4, part, 1, 0, 0, 1)

    def relay_last(part):
        arrived(5, part)
        send_grad(6, part, 2, 0, 0, 1)

    for part in range(PARTS):
        send_grad(0, part, 0, 0, 0, 1)
        send_grad(1, part, 0, 0, 1, 0)
        send_grad(2, part, 0, 0, 3, 0)
    relay_y(0)
    send_near(1)
    send_near(3)
    relay_y(1)
    relay_x(0, 0)
    relay_y(2)
    relay_x(1, 0)
    send_near(2)
    relay_x(2, 0)
    relay_x(3, 0)
    send_swap(0)
    relay_late(3)
    relay_x(0, 1)
    send_swap(1)
    send_swap(3)
    relay_x(1, 1)
    relay_last(3)
    send_swap(2)
    relay_x(2, 1)

    top = jnp.full((8, ROWS), -jnp.inf, F32)
    for k in FORTH:
        swap[k].wait_recv()
        for h in range(2):
            kb = kv[k, 0, h].reshape(256, HD)
            s = nt(kb, q_ref[...])
            scores[k, pl.ds(h * 256, 256)] = s
            top = jnp.maximum(top, jnp.max(s.reshape(32, 8, ROWS), axis=0))
    shift = jnp.max(top, axis=0, keepdims=True) * (FACTOR * LOG2E)
    total = jnp.zeros((8, ROWS), F32)
    acc_t = jnp.zeros((HD, ROWS), F32)
    for k in FORTH:
        for h in range(2):
            vb = kv[k, 1, h].reshape(256, HD)
            e = jnp.exp2(scores[k, pl.ds(h * 256, 256)] * (FACTOR * LOG2E) - shift)
            total = total + jnp.sum(e.reshape(32, 8, ROWS), axis=0)
            eb = e.astype(BF16)
            probs[k, pl.ds(h * 256, 256)] = eb
            acc_t = acc_t + tn(vb, eb)
    inverse = 1.0 / jnp.sum(total, axis=0, keepdims=True)
    att_t[...] = (acc_t * inverse).astype(BF16)

    for part in range(PARTS):
        for i in range(7):
            arrived(i, part)
    x_t = jnp.zeros((HD, ROWS), F32)
    for b in range(8):
        x_t = x_t + nt(w_ref[:, b * 128 : (b + 1) * 128], gall[b])
    x_t = x_t * inverse
    delta = jnp.sum(x_t * att_t[...].astype(F32), axis=0, keepdims=True)
    da_t[...] = x_t.astype(BF16)
    da[...] = x_t.T.astype(BF16)

    for b in range(8):
        part_w = nn(att_t[...], gall[b]).T
        for j in range(8):
            back, o = (z - (2 * b + j // 4) + 16) % 16, j % 4
            i = back % 4
            k = ((back + i // 3) // 4) % 4
            spot = acc.at[k, (core + o % 2) % 2, (yl + o // 2) % 2, i]
            spot[pl.ds(2 * KEYS, 16)] = part_w[j * 16 : (j + 1) * 16]

    dq_t[...] = jnp.zeros((HD, ROWS), F32)
    first, merged, last = {}, {}, {}

    def compute(k):
        for h in range(2):
            kb = kv[k, 0, h].reshape(256, HD)
            vb = kv[k, 1, h].reshape(256, HD)
            pb = probs[k, pl.ds(h * 256, 256)]
            ds = (pb.astype(F32) * (nn(vb, da_t[...]) - delta)).astype(BF16)
            acc[k, h, :, :, pl.ds(0, KEYS)] = (nn(ds, q_ref[...]) * FACTOR).reshape(2, 4, KEYS, HD)
            acc[k, h, :, :, pl.ds(KEYS, KEYS)] = nn(pb, da[...]).reshape(2, 4, KEYS, HD)
            dq_t[...] += tn(kb, ds)
        s1[k] = acc[k, 1].astype(BF16)
        first[k] = go(copy(s1.at[k], r1.at[k], c1_s.at[k], c1_r.at[k], on_ctx(dc=1)))

    def spread(k):
        first[k].wait_recv()
        for e, i in SPOTS:
            s3[k, e, i] = (acc[k, 0, e, i] + r1[k, e, i].astype(F32)).astype(BF16)
            merged[k, e, i] = go(
                copy(
                    s3.at[k, e, i],
                    r3.at[k, e, i],
                    m_s.at[k, e, i],
                    m_r.at[k, e, i],
                    on_ctx(dz=16 - NEAR[i], dy=e),
                )
            )

    def collect(k):
        total = acc[k, 0, 0, 0] + r1[k, 0, 0].astype(F32)
        for e, i in SPOTS:
            merged[k, e, i].wait_recv()
            total = total + r3[k, e, i].astype(F32)
        if k:
            s4[k] = total.astype(BF16)
            last[k] = go(copy(s4.at[k], r4.at[k], z4_s.at[k], z4_r.at[k], on_ctx(dz=16 - 4 * k)))
        return total

    compute(2)
    compute(1)
    spread(2)
    compute(3)
    spread(1)
    compute(0)
    spread(3)
    collect(2)
    spread(0)
    collect(1)
    collect(3)
    dq_ref[...] = (dq_t[...] * FACTOR).T.astype(BF16)
    mine = collect(0)
    for k in (1, 3, 2):
        last[k].wait_recv()
        mine = mine + r4[k].astype(F32)
    dk_ref[...] = mine[0:KEYS].astype(BF16)
    dv_ref[...] = mine[KEYS : 2 * KEYS].astype(BF16)
    dw_ref[...] = mine[2 * KEYS : SLOT]
    for c in sends:
        c.wait_send()


def local(queries, audio_keys, audio_values, grad_output, out_weight):
    vmem = pl.BlockSpec(memory_space=pltpu.VMEM)
    anywhere = pl.BlockSpec(memory_space=pl.ANY)
    dma = lambda *n: pltpu.SemaphoreType.DMA(n)
    scratch = [
        pltpu.VMEM((ROWS, HD), BF16),
        pltpu.VMEM((HD, 8 * HD), BF16),
        pltpu.VMEM((4, 2, 2, 2, 4, KEYS, HD), BF16),
        pltpu.VMEM((8, ROWS, 128), BF16),
        pltpu.VMEM((4, CHUNK, ROWS), F32),
        pltpu.VMEM((4, CHUNK, ROWS), BF16),
        pltpu.VMEM((HD, ROWS), BF16),
        pltpu.VMEM((HD, ROWS), BF16),
        pltpu.VMEM((ROWS, HD), BF16),
        pltpu.VMEM((HD, ROWS), F32),
        pltpu.VMEM((4, 2, 2, 4, SLOT, HD), F32),
        pltpu.VMEM((4, 2, 4, SLOT, HD), BF16),
        pltpu.VMEM((4, 2, 4, SLOT, HD), BF16),
        pltpu.VMEM((4, 2, 4, SLOT, HD), BF16),
        pltpu.VMEM((4, 2, 4, SLOT, HD), BF16),
        pltpu.VMEM((4, SLOT, HD), BF16),
        pltpu.VMEM((4, SLOT, HD), BF16),
        dma(5), dma(4), dma(4), dma(4, 2, 4), dma(4, 2, 4), dma(4), dma(4), dma(7, PARTS), dma(7, PARTS),
        dma(4), dma(4), dma(4, 2, 4), dma(4, 2, 4), dma(4), dma(4),
    ]
    shapes = (
        jax.ShapeDtypeStruct((ROWS, HD), BF16),
        jax.ShapeDtypeStruct((32, HD), BF16),
        jax.ShapeDtypeStruct((32, HD), BF16),
        jax.ShapeDtypeStruct((16, HD), F32),
    )
    dq, dk, dv, dw = pl.pallas_call(
        kernel,
        out_shape=shapes,
        in_specs=[anywhere] * 5,
        out_specs=(vmem,) * 4,
        scratch_shapes=scratch,
        compiler_params=pltpu.CompilerParams(
            collective_id=0, has_side_effects=True, vmem_limit_bytes=56 * 2**20
        ),
    )(queries, audio_keys, audio_values, grad_output, out_weight)
    return dq, dk, dv, dw.T


def solution(mesh):
    return jax.shard_map(
        local,
        mesh=mesh,
        in_specs=(P("ctx", "tp"), P("ctx", "tp"), P("ctx", "tp"), P("ctx", "tp"), P("tp", None)),
        out_specs=(P("ctx", "tp"), P("ctx", "tp"), P("ctx", "tp"), P("tp", "ctx")),
        check_vma=False,
    )
```

time: 80.8 us -> 64.6 us (0.80)
  Pallas kernels: 71.9 us -> 59 us
  local copies, waits for them, and re-layouts: 6.73 us -> 3.68 us
    pallas_call x1, Pallas kernels: 71.9 us -> 59 us  [local(): pl.pallas_call(kernel, out_shape=shapes, in_specs=[anywhere] * 5, out_spe...]
    unnamed x14 -> x10, local copies, waits for them, and re-layouts: 6.73 us -> 3.68 us
where the time goes in v2:
time: 64.6 us; the launch traced here: 63.3 us
  Pallas kernels  59 us (91%)
  local copies, waits for them, and re-layouts  3.68 us (6%)
  between operations  0.65 us (1%)
    pallas_call x1, Pallas kernels, local(): pl.pallas_call(kernel, out_shape=shapes, in_specs=[anywhere] * 5, out_spe...  59 us
    unnamed x10, local copies, waits for them, and re-layouts  3.68 us

profile of v2, /device:TPU:6, one launch (start us, length us, event | category | flops | bytes accessed | tf_op | source)
XLA Modules:
  0.0 63.3 jit_solution(7783654391522754859)
XLA Ops:
  0.6 59.0 %shard_map.84 = (bf16[1024,128]{1,0:T(8,128)(2,1)}, bf16[32,128]{1,0:T(8,128)(2,1)}, bf16[32,128]{1,0:T(8,128)(2,1)}, f32[16,128]{1,0:T(8,128)}) custom-call(bf16[1024,128]{1,0:T(8,128)(2,1)} %q_hbm.1, bf16[32,128]{1,0:T(8,128)(2,1)} %k_hbm.1, bf16[32,128]{1,0:T(8,128)(2,1)} %v_hbm.1, bf16[1024,128]{1,0:T(8,128)(2,1)} %g_hbm.1, bf16[128,1024]{1,0:T(8,128)(2,1)} %w_hbm.1), custom_call_target="tpu_custom_call" | custom-call | tf_op jit(solution)/shard_map/pallas_call | solution.py:315
  59.7 0.0 copy-start.2
  59.7 1.7 %copy.13 = bf16[1024,128]{1,0:T(8,128)(2,1)} copy(bf16[1024,128]{1,0:T(8,128)(2,1)} %get-tuple-element.16) | data formatting | bytes 524288
  61.3 0.0 copy-done.2
  61.3 0.0 copy-start.1
  61.3 0.6 copy.14
  61.9 0.1 copy-done.1
  62.0 0.0 copy-start
  62.0 0.6 copy.15
  62.6 0.1 copy-done
  62.8 0.6 copy.16
Async XLA Ops:
  59.7 1.7 %copy-start.2 = (bf16[32,128]{1,0:T(8,128)(2,1)S(1)}, bf16[32,128]{1,0:T(8,128)(2,1)}, u32[]{:S(2)}) copy-start(bf16[32,128]{1,0:T(8,128)(2,1)} %get-tuple-element.17) | copy-start | bytes 24580
  61.3 0.7 %copy-start.1 = (bf16[32,128]{1,0:T(8,128)(2,1)S(1)}, bf16[32,128]{1,0:T(8,128)(2,1)}, u32[]{:S(2)}) copy-start(bf16[32,128]{1,0:T(8,128)(2,1)} %get-tuple-element.18) | copy-start | bytes 24580
  62.0 0.7 %copy-start = (f32[16,128]{1,0:T(8,128)S(1)}, f32[16,128]{1,0:T(8,128)}, u32[]{:S(2)}) copy-start(f32[16,128]{1,0:T(8,128)} %get-tuple-element.11) | copy-start | bytes 24580

commit v3 on v2

--- a/solution.py
+++ b/solution.py
@@ -18,9 +18,10 @@
 PART = ROWS // PARTS
 FACTOR = 1.0 / math.sqrt(HD)
 LOG2E = math.log2(math.e)
-NEAR = (0, 1, 2, 15)
+NEAR = ((0, 1, 2, 15), (0, 1, 14, 15))
 FORTH = (0, 1, 3, 2)
 BACK = (2, 1, 3, 0)
+PART_ORDER = (0, 1, 2, 3)
 SPOTS = [(e, i) for i in (2, 1, 3, 0) for e in range(2) if i or e]
 
 
@@ -38,9 +39,9 @@
 
 def kernel(
     q_hbm, k_hbm, v_hbm, g_hbm, w_hbm,
-    dq_ref, dk_ref, dv_ref, dw_ref,
+    dq_hbm, dk_hbm, dv_hbm, dw_hbm,
     q_ref, w_ref, kv, gall, scores, probs, att_t, da_t, da, dq_t, acc,
-    s1, r1, s3, r3, s4, r4,
+    s1, r1, s3, r3, s4, r4, gw, delta_ref, dq_ref, dk_ref, dv_ref, dw_ref, out_s,
     in_s, far_s, far_r, near_s, near_r, ca_s, ca_r, g_s, g_r,
     c1_s, c1_r, m_s, m_r, z4_s, z4_r,
 ):
@@ -72,7 +73,7 @@
     barrier = pltpu.get_barrier_semaphore()
     greeted = [on_ctx(dc=1), on_ctx(dy=1)]
     greeted += [on_ctx(dz=d, dy=e) for d in (1, 15, 2, 14) for e in range(2)]
-    greeted += [on_ctx(dz=d) for d in (4, 8, 12)]
+    greeted += [on_ctx(dz=4), on_ctx(dz=12)]
     greeted += [on_tp(0, 1), on_tp(1, 0), on_tp(3, 0)]
     for there in greeted:
         pl.semaphore_signal(barrier, inc=1, device_id=there, device_id_type=MESH)
@@ -87,15 +88,20 @@
         sends.append(c)
         return c
 
-    far = {
-        k: go(copy(own, kv.at[k, :, 0, 0, 0], far_s.at[k], far_r.at[k], on_ctx(dz=4 * k)))
-        for k in (2, 1, 3)
-    }
+    far = {}
+
+    def send_far(k, src, dz):
+        far[k] = go(copy(src, kv.at[k, :, 0, 0, 0], far_s.at[k], far_r.at[k], on_ctx(dz=dz)))
+
+    send_far(1, own, 4)
+    send_far(3, own, 12)
     near = {}
 
     def send_near(k):
         if k:
             far[k].wait_recv()
+        if k == 1:
+            send_far(2, kv.at[1, :, 0, 0, 0], 4)
         for e, i in SPOTS:
             near[k, e, i] = go(
                 copy(
@@ -103,7 +109,7 @@
                     kv.at[k, :, 0, e, i],
                     near_s.at[k, e, i],
                     near_r.at[k, e, i],
-                    on_ctx(dz=NEAR[i], dy=e),
+                    on_ctx(dz=NEAR[e][i], dy=e),
                 )
             )
 
@@ -199,24 +205,30 @@
     inverse = 1.0 / jnp.sum(total, axis=0, keepdims=True)
     att_t[...] = (acc_t * inverse).astype(BF16)
 
-    for part in range(PARTS):
+    for part in PART_ORDER:
         for i in range(7):
             arrived(i, part)
-    x_t = jnp.zeros((HD, ROWS), F32)
+        rows = pl.ds(part * PART, PART)
+        x_t = jnp.zeros((HD, PART), F32)
+        for b in range(8):
+            x_t = x_t + nt(w_ref[:, b * 128 : (b + 1) * 128], gall[b, rows])
+            term = nn(att_t[:, rows], gall[b, rows])
+            if part == PART_ORDER[0]:
+                gw[b] = term
+            else:
+                gw[b] += term
+        x_t = x_t * inverse[:, part * PART : (part + 1) * PART]
+        delta_ref[:, rows] = jnp.sum(x_t * att_t[:, rows].astype(F32), axis=0, keepdims=True)
+        da_t[:, rows] = x_t.astype(BF16)
+        da[rows] = x_t.T.astype(BF16)
+    delta = delta_ref[...]
     for b in range(8):
-        x_t = x_t + nt(w_ref[:, b * 128 : (b + 1) * 128], gall[b])
-    x_t = x_t * inverse
-    delta = jnp.sum(x_t * att_t[...].astype(F32), axis=0, keepdims=True)
-    da_t[...] = x_t.astype(BF16)
-    da[...] = x_t.T.astype(BF16)
-
-    for b in range(8):
-        part_w = nn(att_t[...], gall[b]).T
+        part_w = gw[b].T
         for j in range(8):
             back, o = (z - (2 * b + j // 4) + 16) % 16, j % 4
-            i = back % 4
-            k = ((back + i // 3) // 4) % 4
-            spot = acc.at[k, (core + o % 2) % 2, (yl + o // 2) % 2, i]
+            i, e = back % 4, (yl + o // 2) % 2
+            k = ((back + i // 3 + 2 * e * (i // 2 - i // 3)) // 4) % 4
+            spot = acc.at[k, (core + o % 2) % 2, e, i]
             spot[pl.ds(2 * KEYS, 16)] = part_w[j * 16 : (j + 1) * 16]
 
     dq_t[...] = jnp.zeros((HD, ROWS), F32)
@@ -244,7 +256,7 @@
                     r3.at[k, e, i],
                     m_s.at[k, e, i],
                     m_r.at[k, e, i],
-                    on_ctx(dz=16 - NEAR[i], dy=e),
+                    on_ctx(dz=16 - NEAR[e][i], dy=e),
                 )
             )
 
@@ -253,9 +265,13 @@
         for e, i in SPOTS:
             merged[k, e, i].wait_recv()
             total = total + r3[k, e, i].astype(F32)
+        if k == 1:
+            last[2].wait_recv()
+            total = total + r4[2].astype(F32)
         if k:
             s4[k] = total.astype(BF16)
-            last[k] = go(copy(s4.at[k], r4.at[k], z4_s.at[k], z4_r.at[k], on_ctx(dz=16 - 4 * k)))
+            there = on_ctx(dz=4 if k == 3 else 12)
+            last[k] = go(copy(s4.at[k], r4.at[k], z4_s.at[k], z4_r.at[k], there))
         return total
 
     compute(2)
@@ -267,22 +283,47 @@
     spread(3)
     collect(2)
     spread(0)
-    collect(1)
     collect(3)
     dq_ref[...] = (dq_t[...] * FACTOR).T.astype(BF16)
+    results = [
+        pltpu.make_async_copy(a, b, out_s.at[i])
+        for i, (a, b) in enumerate(
+            ((dq_ref, dq_hbm), (dk_ref, dk_hbm), (dv_ref, dv_hbm), (dw_ref, dw_hbm))
+        )
+    ]
+    results[0].start()
+    collect(1)
     mine = collect(0)
-    for k in (1, 3, 2):
+    for k in (3, 1):
         last[k].wait_recv()
         mine = mine + r4[k].astype(F32)
     dk_ref[...] = mine[0:KEYS].astype(BF16)
     dv_ref[...] = mine[KEYS : 2 * KEYS].astype(BF16)
     dw_ref[...] = mine[2 * KEYS : SLOT]
+    for c in results[1:]:
+        c.start()
     for c in sends:
         c.wait_send()
+    for c in results:
+        c.wait()
+
+
+def finish(*refs):
+    n = (len(refs) - 2) // 3
+    ins, outs, held = refs[:n], refs[n : 2 * n], refs[2 * n : 3 * n]
+    came, went = refs[3 * n :]
+    first = [pltpu.make_async_copy(ins[i], held[i], came.at[i]) for i in range(n)]
+    second = [pltpu.make_async_copy(held[i], outs[i], went.at[i]) for i in range(n)]
+    for c in first:
+        c.start()
+    for a, b in zip(first, second):
+        a.wait()
+        b.start()
+    for c in second:
+        c.wait()
 
 
 def local(queries, audio_keys, audio_values, grad_output, out_weight):
-    vmem = pl.BlockSpec(memory_space=pltpu.VMEM)
     anywhere = pl.BlockSpec(memory_space=pl.ANY)
     dma = lambda *n: pltpu.SemaphoreType.DMA(n)
     scratch = [
@@ -303,6 +344,13 @@
         pltpu.VMEM((4, 2, 4, SLOT, HD), BF16),
         pltpu.VMEM((4, SLOT, HD), BF16),
         pltpu.VMEM((4, SLOT, HD), BF16),
+        pltpu.VMEM((8, HD, HD), F32),
+        pltpu.VMEM((1, ROWS), F32),
+        pltpu.VMEM((ROWS, HD), BF16),
+        pltpu.VMEM((KEYS, HD), BF16),
+        pltpu.VMEM((KEYS, HD), BF16),
+        pltpu.VMEM((16, HD), F32),
+        dma(4),
         dma(5), dma(4), dma(4), dma(4, 2, 4), dma(4, 2, 4), dma(4), dma(4), dma(7, PARTS), dma(7, PARTS),
         dma(4), dma(4), dma(4, 2, 4), dma(4, 2, 4), dma(4), dma(4),
     ]
@@ -312,16 +360,23 @@
         jax.ShapeDtypeStruct((32, HD), BF16),
         jax.ShapeDtypeStruct((16, HD), F32),
     )
-    dq, dk, dv, dw = pl.pallas_call(
+    results = pl.pallas_call(
         kernel,
         out_shape=shapes,
         in_specs=[anywhere] * 5,
-        out_specs=(vmem,) * 4,
+        out_specs=(anywhere,) * 4,
         scratch_shapes=scratch,
         compiler_params=pltpu.CompilerParams(
             collective_id=0, has_side_effects=True, vmem_limit_bytes=56 * 2**20
         ),
     )(queries, audio_keys, audio_values, grad_output, out_weight)
+    dq, dk, dv, dw = pl.pallas_call(
+        finish,
+        out_shape=shapes,
+        in_specs=[anywhere] * 4,
+        out_specs=(anywhere,) * 4,
+        scratch_shapes=[pltpu.VMEM(x.shape, x.dtype) for x in shapes] + [dma(4), dma(4)],
+    )(*results)
     return dq, dk, dv, dw.T
 
 

time: 64.6 us -> 59.3 us (0.918)
  local copies, waits for them, and re-layouts: 3.68 us -> 0 us
  Pallas kernels: 59 us -> 58 us
    unnamed x10 -> x0, local copies, waits for them, and re-layouts: 3.68 us -> none
    pallas_call x1, Pallas kernels: 59 us -> 56.2 us  [local(): pl.pallas_call(kernel, out_shape=shapes, in_specs=[anywhere] * 5, out_spe...]
    pallas_call x0 -> x1, Pallas kernels: none -> 1.73 us  [local(): pl.pallas_call(finish, out_shape=shapes, in_specs=[anywhere] * 4, out_spe...]
where the time goes in v3:
time: 59.3 us; the launch traced here: 58.6 us
  Pallas kernels  58 us (98%)
  between operations  0.64 us (1%)
    pallas_call x1, Pallas kernels, local(): pl.pallas_call(kernel, out_shape=shapes, in_specs=[anywhere] * 5, out_spe...  56.2 us
    pallas_call x1, Pallas kernels, local(): pl.pallas_call(finish, out_shape=shapes, in_specs=[anywhere] * 4, out_spe...  1.73 us

profile of v3, /device:TPU:6, one launch (start us, length us, event | category | flops | bytes accessed | tf_op | source)
XLA Modules:
  0.0 58.6 jit_solution(5174357731610308585)
XLA Ops:
  0.6 56.2 %shard_map.84 = (bf16[1024,128]{1,0:T(8,128)(2,1)}, bf16[32,128]{1,0:T(8,128)(2,1)}, bf16[32,128]{1,0:T(8,128)(2,1)}, f32[16,128]{1,0:T(8,128)}) custom-call(bf16[1024,128]{1,0:T(8,128)(2,1)} %q_hbm.1, bf16[32,128]{1,0:T(8,128)(2,1)} %k_hbm.1, bf16[32,128]{1,0:T(8,128)(2,1)} %v_hbm.1, bf16[1024,128]{1,0:T(8,128)(2,1)} %g_hbm.1, bf16[128,1024]{1,0:T(8,128)(2,1)} %w_hbm.1), custom_call_target="tpu_custom_call" | custom-call | tf_op jit(solution)/shard_map/pallas_call | solution.py:363
  56.9 1.7 %shard_map.85 = (bf16[1024,128]{1,0:T(8,128)(2,1)}, bf16[32,128]{1,0:T(8,128)(2,1)}, bf16[32,128]{1,0:T(8,128)(2,1)}, f32[16,128]{1,0:T(8,128)}) custom-call(bf16[1024,128]{1,0:T(8,128)(2,1)} %get-tuple-element.12.refs_0_, bf16[32,128]{1,0:T(8,128)(2,1)} %get-tuple-element.13.refs_1_, bf16[32,128]{1,0:T(8,128)(2,1)} %get-tuple-element.14.refs_2_, ...), custom_call_target="tpu_custom_call" | custom-call | tf_op jit(solution)/shard_map/pallas_call | solution.py:373

commit v4 on v3

--- a/solution.py
+++ b/solution.py
@@ -39,9 +39,9 @@
 
 def kernel(
     q_hbm, k_hbm, v_hbm, g_hbm, w_hbm,
-    dq_hbm, dk_hbm, dv_hbm, dw_hbm,
+    dq_hbm, mine_hbm, got_hbm,
     q_ref, w_ref, kv, gall, scores, probs, att_t, da_t, da, dq_t, acc,
-    s1, r1, s3, r3, s4, r4, gw, delta_ref, dq_ref, dk_ref, dv_ref, dw_ref, out_s,
+    s1, r1, s3, r3, s4, r4, gw, delta_ref, dq_ref, mine_ref, out_s,
     in_s, far_s, far_r, near_s, near_r, ca_s, ca_r, g_s, g_r,
     c1_s, c1_r, m_s, m_r, z4_s, z4_r,
 ):
@@ -120,7 +120,6 @@
             near[k, e, i].wait_recv()
         swap[k] = go(copy(kv.at[k, :, 0], kv.at[k, :, 1], ca_s.at[k], ca_r.at[k], on_ctx(dc=1)))
 
-    send_near(0)
 
     gc = {}
 
@@ -163,6 +162,7 @@
         send_grad(0, part, 0, 0, 0, 1)
         send_grad(1, part, 0, 0, 1, 0)
         send_grad(2, part, 0, 0, 3, 0)
+    send_near(0)
     relay_y(0)
     send_near(1)
     send_near(3)
@@ -267,11 +267,12 @@
             total = total + r3[k, e, i].astype(F32)
         if k == 1:
             last[2].wait_recv()
-            total = total + r4[2].astype(F32)
+            total = total + r4[0].astype(F32)
         if k:
             s4[k] = total.astype(BF16)
             there = on_ctx(dz=4 if k == 3 else 12)
-            last[k] = go(copy(s4.at[k], r4.at[k], z4_s.at[k], z4_r.at[k], there))
+            lands = r4.at[0] if k == 2 else got_hbm.at[k // 2]
+            last[k] = go(copy(s4.at[k], lands, z4_s.at[k], z4_r.at[k], there))
         return total
 
     compute(2)
@@ -286,39 +287,53 @@
     collect(3)
     dq_ref[...] = (dq_t[...] * FACTOR).T.astype(BF16)
     results = [
-        pltpu.make_async_copy(a, b, out_s.at[i])
-        for i, (a, b) in enumerate(
-            ((dq_ref, dq_hbm), (dk_ref, dk_hbm), (dv_ref, dv_hbm), (dw_ref, dw_hbm))
-        )
+        pltpu.make_async_copy(dq_ref, dq_hbm, out_s.at[0]),
+        pltpu.make_async_copy(mine_ref, mine_hbm, out_s.at[1]),
     ]
     results[0].start()
     collect(1)
-    mine = collect(0)
+    mine_ref[...] = collect(0)
+    results[1].start()
     for k in (3, 1):
         last[k].wait_recv()
-        mine = mine + r4[k].astype(F32)
-    dk_ref[...] = mine[0:KEYS].astype(BF16)
-    dv_ref[...] = mine[KEYS : 2 * KEYS].astype(BF16)
-    dw_ref[...] = mine[2 * KEYS : SLOT]
-    for c in results[1:]:
-        c.start()
     for c in sends:
         c.wait_send()
     for c in results:
         c.wait()
 
 
-def finish(*refs):
-    n = (len(refs) - 2) // 3
-    ins, outs, held = refs[:n], refs[n : 2 * n], refs[2 * n : 3 * n]
-    came, went = refs[3 * n :]
-    first = [pltpu.make_async_copy(ins[i], held[i], came.at[i]) for i in range(n)]
-    second = [pltpu.make_async_copy(held[i], outs[i], went.at[i]) for i in range(n)]
+def finish(dq_in, mine_in, got_in, dq_out, dk_out, dv_out, dw_out, dq, mine, got, dk, dv, dw, came, went):
+    pieces = [pl.ds(i * PART, PART) for i in range(PARTS)]
+    first = [
+        pltpu.make_async_copy(mine_in, mine, came.at[0]),
+        pltpu.make_async_copy(got_in, got, came.at[1]),
+    ]
+    first += [
+        pltpu.make_async_copy(dq_in.at[rows], dq.at[rows], came.at[2 + i])
+        for i, rows in enumerate(pieces)
+    ]
     for c in first:
         c.start()
-    for a, b in zip(first, second):
-        a.wait()
-        b.start()
+    second = [
+        pltpu.make_async_copy(dk, dk_out, went.at[0]),
+        pltpu.make_async_copy(dv, dv_out, went.at[1]),
+        pltpu.make_async_copy(dw, dw_out, went.at[2]),
+    ]
+    second += [
+        pltpu.make_async_copy(dq.at[rows], dq_out.at[rows], went.at[3 + i])
+        for i, rows in enumerate(pieces)
+    ]
+    first[0].wait()
+    first[1].wait()
+    total = mine[...] + got[1].astype(F32) + got[0].astype(F32)
+    dk[...] = total[0:KEYS].astype(BF16)
+    dv[...] = total[KEYS : 2 * KEYS].astype(BF16)
+    dw[...] = total[2 * KEYS : SLOT]
+    for c in second[:3]:
+        c.start()
+    for i in range(PARTS):
+        first[2 + i].wait()
+        second[3 + i].start()
     for c in second:
         c.wait()
 
@@ -343,14 +358,12 @@
         pltpu.VMEM((4, 2, 4, SLOT, HD), BF16),
         pltpu.VMEM((4, 2, 4, SLOT, HD), BF16),
         pltpu.VMEM((4, SLOT, HD), BF16),
-        pltpu.VMEM((4, SLOT, HD), BF16),
+        pltpu.VMEM((1, SLOT, HD), BF16),
         pltpu.VMEM((8, HD, HD), F32),
         pltpu.VMEM((1, ROWS), F32),
         pltpu.VMEM((ROWS, HD), BF16),
-        pltpu.VMEM((KEYS, HD), BF16),
-        pltpu.VMEM((KEYS, HD), BF16),
-        pltpu.VMEM((16, HD), F32),
-        dma(4),
+        pltpu.VMEM((SLOT, HD), F32),
+        dma(2),
         dma(5), dma(4), dma(4), dma(4, 2, 4), dma(4, 2, 4), dma(4), dma(4), dma(7, PARTS), dma(7, PARTS),
         dma(4), dma(4), dma(4, 2, 4), dma(4, 2, 4), dma(4), dma(4),
     ]
@@ -360,11 +373,16 @@
         jax.ShapeDtypeStruct((32, HD), BF16),
         jax.ShapeDtypeStruct((16, HD), F32),
     )
+    parts = (
+        shapes[0],
+        jax.ShapeDtypeStruct((SLOT, HD), F32),
+        jax.ShapeDtypeStruct((2, SLOT, HD), BF16),
+    )
     results = pl.pallas_call(
         kernel,
-        out_shape=shapes,
+        out_shape=parts,
         in_specs=[anywhere] * 5,
-        out_specs=(anywhere,) * 4,
+        out_specs=(anywhere,) * 3,
         scratch_shapes=scratch,
         compiler_params=pltpu.CompilerParams(
             collective_id=0, has_side_effects=True, vmem_limit_bytes=56 * 2**20
@@ -373,9 +391,10 @@
     dq, dk, dv, dw = pl.pallas_call(
         finish,
         out_shape=shapes,
-        in_specs=[anywhere] * 4,
+        in_specs=[anywhere] * 3,
         out_specs=(anywhere,) * 4,
-        scratch_shapes=[pltpu.VMEM(x.shape, x.dtype) for x in shapes] + [dma(4), dma(4)],
+        scratch_shapes=[pltpu.VMEM(x.shape, x.dtype) for x in parts + shapes[1:]]
+        + [dma(2 + PARTS), dma(3 + PARTS)],
     )(*results)
     return dq, dk, dv, dw.T
 

time: 59.3 us -> 58.5 us (0.987)
  Pallas kernels: 58 us -> 57.2 us
    pallas_call x2, Pallas kernels: 58 us -> 57.2 us  [the longest x1 55.4 us: local(): pl.pallas_call(kernel, out_shape=parts, in_specs=[anywhere] * 5, out_spec...]
where the time goes in v4:
time: 58.5 us; the launch traced here: 57.8 us
  Pallas kernels  57.2 us (98%)
  between operations  0.64 us (1%)
    pallas_call x1, Pallas kernels, local(): pl.pallas_call(kernel, out_shape=parts, in_specs=[anywhere] * 5, out_spec...  55.4 us
    pallas_call x1, Pallas kernels, local(): pl.pallas_call(finish, out_shape=shapes, in_specs=[anywhere] * 3, out_spe...  1.73 us

profile of v4, /device:TPU:6, one launch (start us, length us, event | category | flops | bytes accessed | tf_op | source)
XLA Modules:
  0.0 57.8 jit_solution(830034920169808808)
XLA Ops:
  0.6 55.4 %shard_map.84 = (bf16[1024,128]{1,0:T(8,128)(2,1)}, f32[80,128]{1,0:T(8,128)}, bf16[2,80,128]{2,1,0:T(8,128)(2,1)}) custom-call(bf16[1024,128]{1,0:T(8,128)(2,1)} %q_hbm.1, bf16[32,128]{1,0:T(8,128)(2,1)} %k_hbm.1, bf16[32,128]{1,0:T(8,128)(2,1)} %v_hbm.1, bf16[1024,128]{1,0:T(8,128)(2,1)} %g_hbm.1, bf16[128,1024]{1,0:T(8,128)(2,1)} %w_hbm.1), custom_call_target="tpu_custom_call" | custom-call | tf_op jit(solution)/shard_map/pallas_call | solution.py:381
  56.1 1.7 %shard_map.85 = (bf16[1024,128]{1,0:T(8,128)(2,1)}, bf16[32,128]{1,0:T(8,128)(2,1)}, bf16[32,128]{1,0:T(8,128)(2,1)}, f32[16,128]{1,0:T(8,128)}) custom-call(bf16[1024,128]{1,0:T(8,128)(2,1)} %get-tuple-element.11.dq_in, f32[80,128]{1,0:T(8,128)} %get-tuple-element.12.mine_in, bf16[2,80,128]{2,1,0:T(8,128)(2,1)} %get-tuple-element.13.got_in), custom_call_target="tpu_custom_call" | custom-call | tf_op jit(solution)/shard_map/pallas_call | solution.py:391

commit v5 on v4

--- a/solution.py
+++ b/solution.py
@@ -163,25 +163,25 @@
         send_grad(1, part, 0, 0, 1, 0)
         send_grad(2, part, 0, 0, 3, 0)
     send_near(0)
+    send_near(1)
     relay_y(0)
-    send_near(1)
     send_near(3)
     relay_y(1)
     relay_x(0, 0)
     relay_y(2)
+    send_near(2)
     relay_x(1, 0)
-    send_near(2)
     relay_x(2, 0)
     relay_x(3, 0)
+    relay_late(3)
     send_swap(0)
-    relay_late(3)
     relay_x(0, 1)
     send_swap(1)
+    relay_x(1, 1)
     send_swap(3)
-    relay_x(1, 1)
     relay_last(3)
+    relay_x(2, 1)
     send_swap(2)
-    relay_x(2, 1)
 
     top = jnp.full((8, ROWS), -jnp.inf, F32)
     for k in FORTH:
@@ -235,6 +235,7 @@
     first, merged, last = {}, {}, {}
 
     def compute(k):
+        held = []
         for h in range(2):
             kb = kv[k, 0, h].reshape(256, HD)
             vb = kv[k, 1, h].reshape(256, HD)
@@ -242,9 +243,11 @@
             ds = (pb.astype(F32) * (nn(vb, da_t[...]) - delta)).astype(BF16)
             acc[k, h, :, :, pl.ds(0, KEYS)] = (nn(ds, q_ref[...]) * FACTOR).reshape(2, 4, KEYS, HD)
             acc[k, h, :, :, pl.ds(KEYS, KEYS)] = nn(pb, da[...]).reshape(2, 4, KEYS, HD)
-            dq_t[...] += tn(kb, ds)
+            held.append((kb, ds))
         s1[k] = acc[k, 1].astype(BF16)
         first[k] = go(copy(s1.at[k], r1.at[k], c1_s.at[k], c1_r.at[k], on_ctx(dc=1)))
+        for kb, ds in held:
+            dq_t[...] += tn(kb, ds)
 
     def spread(k):
         first[k].wait_recv()

time: 58.5 us -> 58.4 us (level)
  no operation moved by 1% of the time
where the time goes in v5:
time: 58.4 us; the launch traced here: 58.2 us
  Pallas kernels  57.6 us (99%)
  between operations  0.64 us (1%)
    pallas_call x1, Pallas kernels, local(): pl.pallas_call(kernel, out_shape=parts, in_specs=[anywhere] * 5, out_spec...  55.8 us
    pallas_call x1, Pallas kernels, local(): pl.pallas_call(finish, out_shape=shapes, in_specs=[anywhere] * 3, out_spe...  1.73 us

profile of v5, /device:TPU:6, one launch (start us, length us, event | category | flops | bytes accessed | tf_op | source)
XLA Modules:
  0.0 58.2 jit_solution(8931990804550409050)
XLA Ops:
  0.6 55.8 %shard_map.84 = (bf16[1024,128]{1,0:T(8,128)(2,1)}, f32[80,128]{1,0:T(8,128)}, bf16[2,80,128]{2,1,0:T(8,128)(2,1)}) custom-call(bf16[1024,128]{1,0:T(8,128)(2,1)} %q_hbm.1, bf16[32,128]{1,0:T(8,128)(2,1)} %k_hbm.1, bf16[32,128]{1,0:T(8,128)(2,1)} %v_hbm.1, bf16[1024,128]{1,0:T(8,128)(2,1)} %g_hbm.1, bf16[128,1024]{1,0:T(8,128)(2,1)} %w_hbm.1), custom_call_target="tpu_custom_call" | custom-call | tf_op jit(solution)/shard_map/pallas_call | solution.py:384
  56.5 1.7 %shard_map.85 = (bf16[1024,128]{1,0:T(8,128)(2,1)}, bf16[32,128]{1,0:T(8,128)(2,1)}, bf16[32,128]{1,0:T(8,128)(2,1)}, f32[16,128]{1,0:T(8,128)}) custom-call(bf16[1024,128]{1,0:T(8,128)(2,1)} %get-tuple-element.11.dq_in, f32[80,128]{1,0:T(8,128)} %get-tuple-element.12.mine_in, bf16[2,80,128]{2,1,0:T(8,128)(2,1)} %get-tuple-element.13.got_in), custom_call_target="tpu_custom_call" | custom-call | tf_op jit(solution)/shard_map/pallas_call | solution.py:394
